TPU v7x, 32 devices: a whole 2x2x4 slice. The times are simulated.
32 devices in a mesh: dp: 16 (over z, x, core), tensor: 2 (over y).
Axes of the slice: x: 2, y: 2, z: 4, core: 2. Of those that a mesh axis runs over, the one named last changes fastest.
Arguments:
- tokens: bfloat16 [16384, 1024], P(('dp', 'tensor')), may hold values from -6 to 6
- segments: int32 [16384], P(('dp', 'tensor')), may hold values from 0 to 4, as said below
- positions: int32 [16384], P(('dp', 'tensor')), may hold values from 0 to 2047, as said below
- query_weight: bfloat16 [1024, 2048], P('dp', 'tensor'), may hold values from -0.1875 to 0.1875
- key_matrix: bfloat16 [1024, 1024], P('dp', 'tensor'), may hold values from -0.1875 to 0.1875
- value_matrix: bfloat16 [1024, 1024], P('dp', 'tensor'), may hold values from -0.1875 to 0.1875
- out_weight: bfloat16 [2048, 1024], P('tensor', 'dp'), may hold values from -1 to 1
- gate_weight: bfloat16 [1024, 3072], P('dp', 'tensor'), may hold values from -0.1875 to 0.1875
- up_weight: bfloat16 [1024, 3072], P('dp', 'tensor'), may hold values from -0.1875 to 0.1875
- down_weight: bfloat16 [3072, 1024], P('tensor', 'dp'), may hold values from -0.109375 to 0.109375
- attn_gain: float32 [1024], replicated, may hold values from 0.1 to 1.9
- query_gain: float32 [128], replicated, may hold values from 0.1 to 1.9
- key_norm_gain: float32 [128], replicated, may hold values from 0.1 to 1.9
- ffn_gain: float32 [1024], replicated, may hold values from 0.1 to 1.9
- out_grad: bfloat16 [16384, 1024], P(('dp', 'tensor')), may hold values from -8 to 8
Outputs:
- layer_out: bfloat16 [16384, 1024], P(('dp', 'tensor'))
- tokens_grad: float32 [16384, 1024], P(('dp', 'tensor'))
- query_weight_grad: float32 [1024, 2048], P('dp', 'tensor')
- key_weight_grad: float32 [1024, 1024], P('dp', 'tensor')
- value_weight_grad: float32 [1024, 1024], P('dp', 'tensor')
- out_weight_grad: float32 [2048, 1024], P('tensor', 'dp')
- gate_weight_grad: float32 [1024, 3072], P('dp', 'tensor')
- up_weight_grad: float32 [1024, 3072], P('dp', 'tensor')
- down_weight_grad: float32 [3072, 1024], P('tensor', 'dp')
- attn_gain_grad: float32 [1024], replicated
- query_gain_grad: float32 [128], replicated
- key_gain_grad: float32 [128], replicated
- ffn_gain_grad: float32 [1024], replicated
Inputs may be any that keep to these rules, and one draw needn't show every extreme that they name: `segments`: within each packed sequence of 1024 tokens the numbers never fall and take each of 0 to 4 on one or more tokens; document 2 begins within the sequence's first 512 tokens and ends within its last 512. `positions`: positions rise by one from token to token within a document; document 2 of every packed sequence ends at position 2047.
All inputs are finite; a program needn't handle non-finite values.
Results may differ from a plain program's by a relative error of at most 0.019.
Values may be sent and summed in bfloat16 or wider, within the bound.
A program may use at most 192 MiB of HBM per device.

v0:
```python
import jax
import jax.numpy as jnp
from jax import lax
from jax.sharding import PartitionSpec as P

EPSILON = 1e-06
ROPE_BASE = 1000000.0
NEGATIVE = -1e30


def root_mean_norm(values, gain_row):
    factor = lax.rsqrt(jnp.mean(values * values, axis=-1, keepdims=True) + EPSILON)
    return values * factor * gain_row


def rotary_apply(values, cosine_table, sine_values):
    middle = values.shape[-1] // 2
    turned = jnp.concatenate([-values[..., middle:], values[..., :middle]], axis=-1)
    return values * cosine_table + turned * sine_values


def tables(places, head_dim):
    middle = head_dim // 2
    powers = jnp.arange(middle, dtype=jnp.float32) * (2.0 / head_dim)
    inverse = jnp.power(ROPE_BASE, -powers)
    angles = places.astype(jnp.float32)[:, None] * inverse[None, :]
    angles = jnp.concatenate([angles, angles], axis=-1)
    return (jnp.cos(angles)[:, None, :], jnp.sin(angles)[:, None, :])


def silu_product(gate_rows, up_rows):
    return jax.nn.silu(gate_rows) * up_rows


def matmul(left_side, right_side):
    return jnp.dot(left_side, right_side, preferred_element_type=jnp.float32)


def left_contract(left_side, right_side):
    return lax.dot_general(
        left_side, right_side, (((0,), (0,)), ((), ())), preferred_element_type=jnp.float32
    )


def right_contract(left_side, right_side):
    return lax.dot_general(
        left_side, right_side, (((1,), (1,)), ((), ())), preferred_element_type=jnp.float32
    )


def tile_mask(q_marks, k_marks, q_start, k_start):
    q_places = q_start + jnp.arange(q_marks.shape[0])
    k_places = k_start + jnp.arange(k_marks.shape[0])
    return (q_marks[:, None] == k_marks[None, :]) & (q_places[:, None] >= k_places[None, :])


def tile_scores(q_block, k_block, allowed, score_scale):
    scores = (
        jnp.einsum("qgsd,kgd->gsqk", q_block, k_block, preferred_element_type=jnp.float32)
        * score_scale
    )
    return jnp.where(allowed, scores, NEGATIVE)


def attend_forward(
    query_rows, key_matrix_rows, value_matrix_rows, row_marks, tile_rows, score_scale
):
    seq_rows, groups, heads_per_group, head_dim = query_rows.shape
    tile_count = seq_rows // tile_rows
    mixed_parts, full_parts, total_parts = ([], [], [])
    for q_index in range(tile_count):
        q_start = q_index * tile_rows
        q_block = query_rows[q_start : q_start + tile_rows]
        q_marks = row_marks[q_start : q_start + tile_rows]
        running = jnp.full((groups, heads_per_group, tile_rows), NEGATIVE, jnp.float32)
        totals = jnp.zeros((groups, heads_per_group, tile_rows), jnp.float32)
        for k_index in range(q_index + 1):
            k_start = k_index * tile_rows
            allowed = tile_mask(q_marks, row_marks[k_start : k_start + tile_rows], q_start, k_start)
            scores = tile_scores(
                q_block, key_matrix_rows[k_start : k_start + tile_rows], allowed, score_scale
            )
            newest = jnp.maximum(running, jnp.max(scores, axis=-1))
            fresh = jnp.where(allowed, jnp.exp(scores - newest[..., None]), 0.0)
            totals = totals * jnp.exp(running - newest) + jnp.sum(fresh, axis=-1)
            running = newest
        log_totals = running + jnp.log(totals)
        upper_sum = jnp.zeros((tile_rows, groups, heads_per_group, head_dim), jnp.float32)
        lower_sum = jnp.zeros((tile_rows, groups, heads_per_group, head_dim), jnp.float32)
        for k_index in range(q_index + 1):
            k_start = k_index * tile_rows
            allowed = tile_mask(q_marks, row_marks[k_start : k_start + tile_rows], q_start, k_start)
            scores = tile_scores(
                q_block, key_matrix_rows[k_start : k_start + tile_rows], allowed, score_scale
            )
            probs_tile = jnp.where(allowed, jnp.exp(scores - log_totals[..., None]), 0.0)
            high_part = probs_tile.astype(jnp.bfloat16)
            low_part = (probs_tile - high_part.astype(jnp.float32)).astype(jnp.bfloat16)
            v_block = value_matrix_rows[k_start : k_start + tile_rows]
            upper_sum = upper_sum + jnp.einsum(
                "gsqk,kgd->qgsd", high_part, v_block, preferred_element_type=jnp.float32
            )
            lower_sum = lower_sum + jnp.einsum(
                "gsqk,kgd->qgsd", low_part, v_block, preferred_element_type=jnp.float32
            )
        mixed_parts.append(upper_sum.astype(jnp.bfloat16))
        full_parts.append(upper_sum + lower_sum)
        total_parts.append(log_totals)
    return (
        jnp.concatenate(mixed_parts, 0),
        jnp.concatenate(full_parts, 0),
        jnp.concatenate(total_parts, -1),
    )


def attend_backward(
    query_rows,
    key_matrix_rows,
    value_matrix_rows,
    row_marks,
    log_totals,
    full_mixed,
    grad_mixed,
    tile_rows,
    score_scale,
):
    seq_rows, groups, heads_per_group, head_dim = query_rows.shape
    tile_count = seq_rows // tile_rows
    delta_rows = jnp.einsum("qgsd,qgsd->gsq", grad_mixed.astype(jnp.float32), full_mixed)
    key_grads = [
        jnp.zeros((tile_rows, groups, head_dim), jnp.float32) for k_index in range(tile_count)
    ]
    value_grads = [
        jnp.zeros((tile_rows, groups, head_dim), jnp.float32) for k_index in range(tile_count)
    ]
    query_grads = []
    for q_index in range(tile_count):
        q_start = q_index * tile_rows
        q_block = query_rows[q_start : q_start + tile_rows]
        grad_block = grad_mixed[q_start : q_start + tile_rows]
        q_marks = row_marks[q_start : q_start + tile_rows]
        part_delta = delta_rows[..., q_start : q_start + tile_rows]
        part_totals = log_totals[..., q_start : q_start + tile_rows]
        query_accum = jnp.zeros((tile_rows, groups, heads_per_group, head_dim), jnp.float32)
        for k_index in range(q_index + 1):
            k_start = k_index * tile_rows
            k_block = key_matrix_rows[k_start : k_start + tile_rows]
            v_block = value_matrix_rows[k_start : k_start + tile_rows]
            allowed = tile_mask(q_marks, row_marks[k_start : k_start + tile_rows], q_start, k_start)
            scores = tile_scores(q_block, k_block, allowed, score_scale)
            probs_tile = jnp.where(allowed, jnp.exp(scores - part_totals[..., None]), 0.0)
            grad_probs = jnp.einsum(
                "qgsd,kgd->gsqk", grad_block, v_block, preferred_element_type=jnp.float32
            )
            grad_scores = (probs_tile * (grad_probs - part_delta[..., None])).astype(jnp.bfloat16)
            query_accum = (
                query_accum
                + jnp.einsum(
                    "gsqk,kgd->qgsd", grad_scores, k_block, preferred_element_type=jnp.float32
                )
                * score_scale
            )
            key_grads[k_index] = (
                key_grads[k_index]
                + jnp.einsum(
                    "gsqk,qgsd->kgd", grad_scores, q_block, preferred_element_type=jnp.float32
                )
                * score_scale
            )
            value_grads[k_index] = value_grads[k_index] + jnp.einsum(
                "gsqk,qgsd->kgd",
                probs_tile.astype(jnp.bfloat16),
                grad_block,
                preferred_element_type=jnp.float32,
            )
        query_grads.append(query_accum)
    return (
        jnp.concatenate(query_grads, 0),
        jnp.concatenate(key_grads, 0),
        jnp.concatenate(value_grads, 0),
    )


def per_device(
    tokens,
    segments,
    positions,
    query_weight,
    key_matrix,
    value_matrix,
    out_weight,
    gate_weight,
    up_weight,
    down_weight,
    attn_gain,
    query_gain,
    key_norm_gain,
    ffn_gain,
    out_grad,
):
    tok_rows = tokens.shape[0]
    head_dim = query_gain.shape[0]
    seq_rows = tok_rows * lax.axis_size("tensor")
    q_heads = query_weight.shape[1] // head_dim
    kv_heads = key_matrix.shape[1] // head_dim
    heads_per_group = q_heads // kv_heads
    tile_rows = min(512, seq_rows)
    score_scale = head_dim ** (-0.5)
    inputs = tokens.astype(jnp.float32)
    unused_first, first_pull = jax.vjp(root_mean_norm, inputs, attn_gain)
    whole_tokens = lax.all_gather(tokens, "tensor", axis=0, tiled=True)
    inputs_whole = whole_tokens.astype(jnp.float32)
    first_rows = root_mean_norm(inputs_whole, attn_gain).astype(jnp.bfloat16)
    row_marks, row_places = (
        lax.all_gather(segments, "tensor", axis=0, tiled=True),
        lax.all_gather(positions, "tensor", axis=0, tiled=True),
    )
    weights = (
        lax.all_gather(query_weight, "dp", axis=0, tiled=True),
        lax.all_gather(key_matrix, "dp", axis=0, tiled=True),
        lax.all_gather(value_matrix, "dp", axis=0, tiled=True),
        lax.all_gather(out_weight, "dp", axis=1, tiled=True),
        lax.all_gather(gate_weight, "dp", axis=0, tiled=True),
        lax.all_gather(up_weight, "dp", axis=0, tiled=True),
        lax.all_gather(down_weight, "dp", axis=1, tiled=True),
    )
    full_query, full_key, full_value, full_out, full_gate, full_up, full_down = weights
    cosine_table, sine_values = tables(row_places, head_dim)

    def head_prep(raw_cols, gain_row):
        heads = raw_cols.reshape(seq_rows, raw_cols.shape[1] // head_dim, head_dim)
        return rotary_apply(root_mean_norm(heads, gain_row), cosine_table, sine_values)

    query_raw = matmul(first_rows, full_query)
    key_unrotated = matmul(first_rows, full_key)
    value_matrix_rows = (
        matmul(first_rows, full_value).astype(jnp.bfloat16).reshape(seq_rows, kv_heads, head_dim)
    )
    query_rot, query_pull = jax.vjp(head_prep, query_raw, query_gain)
    key_rot, key_pull = jax.vjp(head_prep, key_unrotated, key_norm_gain)
    query_rows = query_rot.astype(jnp.bfloat16).reshape(
        seq_rows, kv_heads, heads_per_group, head_dim
    )
    key_matrix_rows = key_rot.astype(jnp.bfloat16)
    mixed_heads, full_mixed, log_totals = attend_forward(
        query_rows, key_matrix_rows, value_matrix_rows, row_marks, tile_rows, score_scale
    )
    mixed_rows = mixed_heads.reshape(seq_rows, q_heads * head_dim)
    hidden = inputs + lax.psum_scatter(
        matmul(mixed_rows, full_out), "tensor", scatter_dimension=0, tiled=True
    )
    second_own = root_mean_norm(hidden, ffn_gain)
    second_rows = lax.all_gather(second_own.astype(jnp.bfloat16), "tensor", axis=0, tiled=True)
    unused_second, second_pull = jax.vjp(root_mean_norm, hidden, ffn_gain)
    gate_rows = matmul(second_rows, full_gate)
    up_rows = matmul(second_rows, full_up)
    activated, act_pull = jax.vjp(silu_product, gate_rows, up_rows)
    act_low = activated.astype(jnp.bfloat16)
    layer_out = (
        hidden
        + lax.psum_scatter(
            matmul(act_low, full_down).astype(jnp.bfloat16),
            "tensor",
            scatter_dimension=0,
            tiled=True,
        ).astype(jnp.float32)
    ).astype(jnp.bfloat16)
    grad_rows = lax.all_gather(out_grad, "tensor", axis=0, tiled=True)
    back_weights = (
        lax.all_gather(query_weight, "dp", axis=0, tiled=True),
        lax.all_gather(key_matrix, "dp", axis=0, tiled=True),
        lax.all_gather(value_matrix, "dp", axis=0, tiled=True),
        lax.all_gather(out_weight, "dp", axis=1, tiled=True),
        lax.all_gather(gate_weight, "dp", axis=0, tiled=True),
        lax.all_gather(up_weight, "dp", axis=0, tiled=True),
        lax.all_gather(down_weight, "dp", axis=1, tiled=True),
    )
    back_query, back_key, back_value, back_out, back_gate, back_up, back_down = back_weights
    grad_act = right_contract(grad_rows, back_down)
    down_grad = left_contract(act_low, grad_rows)
    grad_gate, grad_up = act_pull(grad_act)
    gate_low = grad_gate.astype(jnp.bfloat16)
    up_low = grad_up.astype(jnp.bfloat16)
    gate_grad = left_contract(second_rows, gate_low)
    up_grad = left_contract(second_rows, up_low)
    grad_second = lax.psum_scatter(
        right_contract(gate_low, back_gate) + right_contract(up_low, back_up),
        "tensor",
        scatter_dimension=0,
        tiled=True,
    )
    ffn_grads = (
        lax.psum_scatter(
            gate_grad.astype(jnp.bfloat16), "dp", scatter_dimension=0, tiled=True
        ).astype(jnp.float32),
        lax.psum_scatter(
            up_grad.astype(jnp.bfloat16), "dp", scatter_dimension=0, tiled=True
        ).astype(jnp.float32),
        lax.psum_scatter(
            down_grad.astype(jnp.bfloat16), "dp", scatter_dimension=1, tiled=True
        ).astype(jnp.float32),
    )
    grad_norm, ffn_gain_part = second_pull(grad_second)
    grad_hidden = out_grad.astype(jnp.float32) + grad_norm
    attn_rows = lax.all_gather(grad_hidden.astype(jnp.bfloat16), "tensor", axis=0, tiled=True)
    grad_mixed = right_contract(attn_rows, back_out).astype(jnp.bfloat16)
    out_weight_part = left_contract(mixed_rows, attn_rows)
    grad_query, grad_key, grad_value = attend_backward(
        query_rows,
        key_matrix_rows,
        value_matrix_rows,
        row_marks,
        log_totals,
        full_mixed,
        grad_mixed.reshape(seq_rows, kv_heads, heads_per_group, head_dim),
        tile_rows,
        score_scale,
    )
    query_back, query_gain_part = query_pull(grad_query.reshape(seq_rows, q_heads, head_dim))
    key_back, key_gain_part = key_pull(grad_key)
    query_low = query_back.astype(jnp.bfloat16)
    key_low = key_back.astype(jnp.bfloat16)
    value_low = grad_value.reshape(seq_rows, kv_heads * head_dim).astype(jnp.bfloat16)
    grad_first = lax.psum_scatter(
        (
            right_contract(query_low, back_query)
            + right_contract(key_low, back_key)
            + right_contract(value_low, back_value)
        ).astype(jnp.bfloat16),
        "tensor",
        scatter_dimension=0,
        tiled=True,
    ).astype(jnp.float32)
    attn_grads = (
        lax.psum_scatter(
            left_contract(first_rows, query_low).astype(jnp.bfloat16),
            "dp",
            scatter_dimension=0,
            tiled=True,
        ).astype(jnp.float32),
        lax.psum_scatter(
            left_contract(first_rows, key_low).astype(jnp.bfloat16),
            "dp",
            scatter_dimension=0,
            tiled=True,
        ).astype(jnp.float32),
        lax.psum_scatter(
            left_contract(first_rows, value_low).astype(jnp.bfloat16),
            "dp",
            scatter_dimension=0,
            tiled=True,
        ).astype(jnp.float32),
        lax.psum_scatter(
            out_weight_part.astype(jnp.bfloat16), "dp", scatter_dimension=1, tiled=True
        ).astype(jnp.float32),
    )
    grad_inputs, attn_gain_part = first_pull(grad_first)
    tokens_grad = grad_hidden + grad_inputs
    gain_grads = lax.psum(
        (attn_gain_part, query_gain_part, key_gain_part, ffn_gain_part), ("dp", "tensor")
    )
    return (
        layer_out,
        tokens_grad,
        attn_grads[0],
        attn_grads[1],
        attn_grads[2],
        attn_grads[3],
        ffn_grads[0],
        ffn_grads[1],
        ffn_grads[2],
        gain_grads[0],
        gain_grads[1],
        gain_grads[2],
        gain_grads[3],
    )


def solution(mesh):
    return jax.shard_map(
        per_device,
        mesh=mesh,
        in_specs=(
            P(("dp", "tensor"), None),
            P(("dp", "tensor")),
            P(("dp", "tensor")),
            P("dp", "tensor"),
            P("dp", "tensor"),
            P("dp", "tensor"),
            P("tensor", "dp"),
            P("dp", "tensor"),
            P("dp", "tensor"),
            P("tensor", "dp"),
            P(),
            P(),
            P(),
            P(),
            P(("dp", "tensor"), None),
        ),
        out_specs=(
            P(("dp", "tensor"), None),
            P(("dp", "tensor"), None),
            P("dp", "tensor"),
            P("dp", "tensor"),
            P("dp", "tensor"),
            P("tensor", "dp"),
            P("dp", "tensor"),
            P("dp", "tensor"),
            P("tensor", "dp"),
            P(),
            P(),
            P(),
            P(),
        ),
        check_vma=False,
    )
```

profile of v0, /device:TPU:0, one launch (start us, length us, event | category | flops | bytes accessed | tf_op | source)
XLA Modules:
  0.0 1136.4 jit_solution(8039303094465603463)
XLA Ops:
  10.6 5.5 all-gather.1
  26.4 19.1 %all-gather.14.cloned.1.call-done = bf16[1024,1024]{1,0:T(8,128)(2,1)} async-done(((bf16[512,1024]{1,0:T(8,128)(2,1)}), bf16[1024,1024]{1,0:T(8,128)(2,1)}) %all-gather.14.cloned.1.call-update) | async-done | bytes 2097168 | tf_op jit(solution)/shard_map/all_gather | solution.py:211
  47.6 38.0 %all-gather.18.cloned.1.call-done = bf16[1024,512]{1,0:T(8,128)(2,1)} async-done(((bf16[64,512]{1,0:T(8,128)(2,1)}), bf16[1024,512]{1,0:T(8,128)(2,1)}) %all-gather.18.cloned.1.call-update) | async-done | bytes 1048592 | tf_op jit(solution)/shard_map/all_gather | solution.py:220
  96.1 28.5 %all-gather.16.cloned.1.call-done = bf16[1024,512]{1,0:T(8,128)(2,1)} async-done(((bf16[64,512]{1,0:T(8,128)(2,1)}), bf16[1024,512]{1,0:T(8,128)(2,1)}) %all-gather.16.cloned.1.call-update) | async-done | bytes 1048592 | tf_op jit(solution)/shard_map/all_gather | solution.py:221
  130.7 36.3 %all-gather.20.cloned.1.call-done = bf16[1024,1024]{1,0:T(8,128)(2,1)} async-done(((bf16[64,1024]{1,0:T(8,128)(2,1)}), bf16[1024,1024]{1,0:T(8,128)(2,1)}) %all-gather.20.cloned.1.call-update) | async-done | bytes 2097168 | tf_op jit(solution)/shard_map/all_gather | solution.py:219
  198.1 11.1 all-gather.22.cloned.1.call-done
  209.2 6.1 fusion.99
  216.1 52.4 %reduce-scatter.12.cloned.1.call-done = f32[512,1024]{1,0:T(8,128)} async-done(((f32[1024,1024]{1,0:T(8,128)}), f32[512,1024]{1,0:T(8,128)}) %reduce-scatter.12.cloned.1.call-update) | async-done | bytes 2097168 | tf_op jit(solution)/shard_map/reduce_scatter | solution.py:249
  275.0 41.6 %all-gather.26.cloned.1.call-done = bf16[1024,1536]{1,0:T(8,128)(2,1)} async-done(((bf16[64,1536]{1,0:T(8,128)(2,1)}), bf16[1024,1536]{1,0:T(8,128)(2,1)}) %all-gather.26.cloned.1.call-update) | async-done | bytes 3145744 | tf_op jit(solution)/shard_map/all_gather | solution.py:223
  316.5 34.2 %all-gather.24.cloned.1.call-done = bf16[1024,1024]{1,0:T(8,128)(2,1)} async-done(((bf16[512,1024]{1,0:T(8,128)(2,1)}), bf16[1024,1024]{1,0:T(8,128)(2,1)}) %all-gather.24.cloned.1.call-update) | async-done | bytes 2097168 | tf_op jit(solution)/shard_map/all_gather | solution.py:253
  350.7 8.5 fusion.100
  359.2 39.3 %all-gather.28.cloned.1.call-done = bf16[1024,1536]{1,0:T(8,128)(2,1)} async-done(((bf16[64,1536]{1,0:T(8,128)(2,1)}), bf16[1024,1536]{1,0:T(8,128)(2,1)}) %all-gather.28.cloned.1.call-update) | async-done | bytes 3145744 | tf_op jit(solution)/shard_map/all_gather | solution.py:224
  398.5 8.6 fusion.101
  407.1 24.8 %all-gather.32.cloned.1.call-done = bf16[1024,1024]{1,0:T(8,128)(2,1)} async-done(((bf16[512,1024]{1,0:T(8,128)(2,1)}), bf16[1024,1024]{1,0:T(8,128)(2,1)}) %all-gather.32.cloned.1.call-update) | async-done | bytes 2097168 | tf_op jit(solution)/shard_map/all_gather | solution.py:268
  431.9 47.8 %all-gather.30.cloned.1.call-done = bf16[1536,1024]{0,1:T(8,128)(2,1)} async-done(((bf16[1536,64]{0,1:T(8,128)(2,1)}), bf16[1536,1024]{0,1:T(8,128)(2,1)}) %all-gather.30.cloned.1.call-update) | async-done | bytes 3145744 | tf_op jit(solution)/shard_map/all_gather | solution.py:225
  479.7 11.7 %multiply_convert_fusion = (bf16[1024,1536]{1,0:T(8,128)(2,1)S(1)}, bf16[1024,1536]{1,0:T(8,128)(2,1)S(1)}, bf16[1024,1536]{1,0:T(8,128)(2,1)}) fusion(f32[1024,1536]{1,0:T(8,128)} %fusion.100, f32[1024,1536]{1,0:T(8,128)} %fusion.101, bf16[1024,1024]{1,0:T(8,128)(2,1)} %all-gather.32.cloned.1.call-done, bf16[1536,1024]{0,1:T(8,128)(2,1)} %all-gather.30.cloned.1.call-done), kind=kOutput, calls=%fused_computation.29 | convolution fusion | flops 3246391296 | bytes 27262976 | tf_op jit(solution)/shard_map/dot_general | solution.py:46
  500.7 53.2 %reduce-scatter.16.cloned.1.call-done = f32[512,1024]{1,0:T(8,128)} async-done(((f32[1024,1024]{1,0:T(8,128)}), f32[512,1024]{1,0:T(8,128)}) %reduce-scatter.16.cloned.1.call-update) | async-done | bytes 2097168 | tf_op jit(solution)/shard_map/reduce_scatter | solution.py:286
  559.2 7.9 convolution_convert_fusion.2
  567.2 7.1 convolution_convert_fusion.1
  574.4 5.2 fusion.18
  579.7 7.7 add_bitcast_fusion.1
  596.9 6.1 fusion.23
  603.2 7.0 convolution_bitcast_fusion.4
  686.5 6.6 convolution_convert_fusion.6
  695.1 36.0 %reduce-scatter.30.cloned.1.call-done = bf16[64,1536]{1,0:T(8,128)(2,1)} async-done(((bf16[1024,1536]{1,0:T(8,128)(2,1)}), bf16[64,1536]{1,0:T(8,128)(2,1)}) %reduce-scatter.30.cloned.1.call-update) | async-done | bytes 196624 | tf_op jit(solution)/shard_map/reduce_scatter | solution.py:296
  732.7 67.2 %reduce-scatter.32.cloned.1.call-done = bf16[1536,64]{0,1:T(8,128)(2,1)} async-done(((bf16[1536,1024]{0,1:T(8,128)(2,1)}), bf16[1536,64]{0,1:T(8,128)(2,1)}) %reduce-scatter.32.cloned.1.call-update) | async-done | bytes 196624 | tf_op jit(solution)/shard_map/reduce_scatter | solution.py:299
  801.6 58.1 %reduce-scatter.24.cloned.1.call-done = bf16[64,512]{1,0:T(8,128)(2,1)} async-done(((bf16[1024,512]{1,0:T(8,128)(2,1)}), bf16[64,512]{1,0:T(8,128)(2,1)}) %reduce-scatter.24.cloned.1.call-update) | async-done | bytes 65552 | tf_op jit(solution)/shard_map/reduce_scatter | solution.py:347
  861.2 58.8 %reduce-scatter.22.cloned.1.call-done = bf16[64,512]{1,0:T(8,128)(2,1)} async-done(((bf16[1024,512]{1,0:T(8,128)(2,1)}), bf16[64,512]{1,0:T(8,128)(2,1)}) %reduce-scatter.22.cloned.1.call-update) | async-done | bytes 65552 | tf_op jit(solution)/shard_map/reduce_scatter | solution.py:341
  921.6 62.8 %reduce-scatter.26.cloned.1.call-done = bf16[1024,64]{0,1:T(8,128)(2,1)} async-done(((bf16[1024,1024]{0,1:T(8,128)(2,1)}), bf16[1024,64]{0,1:T(8,128)(2,1)}) %reduce-scatter.26.cloned.1.call-update) | async-done | bytes 131088 | tf_op jit(solution)/shard_map/reduce_scatter | solution.py:353
  986.1 63.0 %reduce-scatter.20.cloned.1.call-done = bf16[64,1024]{1,0:T(8,128)(2,1)} async-done(((bf16[1024,1024]{1,0:T(8,128)(2,1)}), bf16[64,1024]{1,0:T(8,128)(2,1)}) %reduce-scatter.20.cloned.1.call-update) | async-done | bytes 131088 | tf_op jit(solution)/shard_map/reduce_scatter | solution.py:335
  1050.7 32.1 %reduce-scatter.18.cloned.1.call-done = bf16[512,1024]{1,0:T(8,128)(2,1)} async-done(((bf16[1024,1024]{1,0:T(8,128)(2,1)}), bf16[512,1024]{1,0:T(8,128)(2,1)}) %reduce-scatter.18.cloned.1.call-update) | async-done | bytes 1048592 | tf_op jit(solution)/shard_map/reduce_scatter | solution.py:324
  1085.0 39.8 %all-reduce.4 = (f32[1024]{0:T(1024)}, f32[128]{0:T(128)}, f32[128]{0:T(128)}, f32[1024]{0:T(1024)}) all-reduce(f32[1024]{0:T(1024)S(1)} %get-tuple-element.19, f32[128]{0:T(128)S(1)} %get-tuple-element.17, f32[128]{0:T(128)S(1)} %get-tuple-element.15, f32[1024]{0:T(1024)S(1)} %copy-done.84), channel_id=1, replica_groups=mesh['dp'=16,'tensor'=2] {'dp','tensor'}, use_global_device_ids=true, to_apply=%region_27.28 | all-reduce | flops 2304 | bytes 18432 | tf_op jit(solution)/shard_map/psum | solution.py:359
  (366 shorter events, 187.9 us)
Async XLA Ops:
  7.2 38.3 %all-gather.14.cloned.1.call-start = ((), (), s32[]{:S(2)}) async-start(), calls=%async_computation.11 | async-start | bytes 3145728 | tf_op jit(solution)/shard_map/all_gather | solution.py:211
  7.9 77.7 %all-gather.18.cloned.1.call-start = ((), (), s32[]{:S(2)}) async-start(), calls=%async_computation.13 | async-start | bytes 1114112 | tf_op jit(solution)/shard_map/all_gather | solution.py:220
  8.7 116.0 %all-gather.16.cloned.1.call-start = ((), (), s32[]{:S(2)}) async-start(), calls=%async_computation.12 | async-start | bytes 1114112 | tf_op jit(solution)/shard_map/all_gather | solution.py:221
  9.4 157.6 %all-gather.20.cloned.1.call-start = ((), (), s32[]{:S(2)}) async-start(), calls=%async_computation.14 | async-start | bytes 2228224 | tf_op jit(solution)/shard_map/all_gather | solution.py:219
  10.0 199.3 %all-gather.22.cloned.1.call-start = ((), (), s32[]{:S(2)}) async-start(), calls=%async_computation.15 | async-start | bytes 2228224 | tf_op jit(solution)/shard_map/all_gather | solution.py:222
  10.6 258.0 %reduce-scatter.12.cloned.1.call-start = ((), (), s32[]{:S(2)}) async-start(), calls=%async_computation.16 | async-start | bytes 6291456 | tf_op jit(solution)/shard_map/reduce_scatter | solution.py:249
  26.4 583.8 %copy-start.37 = (pred[512,512]{0,1:T(8,128)(4,1)}, pred[512,512]{0,1:T(8,128)(4,1)S(1)}, u32[]{:S(2)}) copy-start(pred[512,512]{0,1:T(8,128)(4,1)S(1)} %get-tuple-element.56) | copy-start | bytes 786436
  47.6 119.5 %copy-start.89 = (f32[1024]{0:T(1024)}, f32[1024]{0:T(1024)S(1)}, u32[]{:S(2)}) copy-start(f32[1024]{0:T(1024)S(1)} %add_rsqrt_fusion) | copy-start | bytes 12292
  215.3 101.2 %all-gather.26.cloned.1.call-start = ((), (), s32[]{:S(2)}) async-start(), calls=%async_computation.18 | async-start | bytes 3342336 | tf_op jit(solution)/shard_map/all_gather | solution.py:223
  216.1 134.6 %all-gather.24.cloned.1.call-start = ((), (), s32[]{:S(2)}) async-start(), calls=%async_computation.17 | async-start | bytes 3145728 | tf_op jit(solution)/shard_map/all_gather | solution.py:253
  271.3 285.5 %copy-start.2 = (f32[512,1024]{1,0:T(8,128)}, f32[512,1024]{1,0:T(8,128)S(1)}, u32[]{:S(2)}) copy-start(f32[512,1024]{1,0:T(8,128)S(1)} %get-tuple-element.28) | copy-start | bytes 6291460
  271.3 285.5 %copy-start.77 = (f32[512]{0:T(512)}, f32[512]{0:T(512)S(1)}, u32[]{:S(2)}) copy-start(f32[512]{0:T(512)S(1)} %fusion.59) | copy-start | bytes 6148
  272.7 125.8 %all-gather.28.cloned.1.call-start = ((), (), s32[]{:S(2)}) async-start(), calls=%async_computation.19 | async-start | bytes 3342336 | tf_op jit(solution)/shard_map/all_gather | solution.py:224
  273.4 158.5 %all-gather.32.cloned.1.call-start = ((), (), s32[]{:S(2)}) async-start(), calls=%async_computation.22 | async-start | bytes 3145728 | tf_op jit(solution)/shard_map/all_gather | solution.py:268
  274.0 205.7 %all-gather.30.cloned.1.call-start = ((), (), s32[]{:S(2)}) async-start(), calls=%async_computation.20 | async-start | bytes 3342336 | tf_op jit(solution)/shard_map/all_gather | solution.py:225
  274.8 279.1 %reduce-scatter.16.cloned.1.call-start = ((), (), s32[]{:S(2)}) async-start(), calls=%async_computation.23 | async-start | bytes 6291456 | tf_op jit(solution)/shard_map/reduce_scatter | solution.py:286
  500.6 96.2 %all-gather.34.cloned.1.call-start = ((), (), s32[]{:S(2)}) async-start(), calls=%async_computation.24 | async-start | bytes 3145728 | tf_op jit(solution)/shard_map/all_gather | solution.py:305
  559.0 134.3 %reduce-scatter.28.cloned.1.call-start = ((), (), s32[]{:S(2)}) async-start(), calls=%async_computation.30 | async-start | bytes 3342336 | tf_op jit(solution)/shard_map/reduce_scatter | solution.py:293
  567.1 163.9 %reduce-scatter.30.cloned.1.call-start = ((), (), s32[]{:S(2)}) async-start(), calls=%async_computation.31 | async-start | bytes 3342336 | tf_op jit(solution)/shard_map/reduce_scatter | solution.py:296
  574.3 225.6 %reduce-scatter.32.cloned.1.call-start = ((), (), s32[]{:S(2)}) async-start(), calls=%async_computation.32 | async-start | bytes 3342336 | tf_op jit(solution)/shard_map/reduce_scatter | solution.py:299
  596.4 263.3 %reduce-scatter.24.cloned.1.call-start = ((), (), s32[]{:S(2)}) async-start(), calls=%async_computation.28 | async-start | bytes 1114112 | tf_op jit(solution)/shard_map/reduce_scatter | solution.py:347
  641.2 278.9 %reduce-scatter.22.cloned.1.call-start = ((), (), s32[]{:S(2)}) async-start(), calls=%async_computation.27 | async-start | bytes 1114112 | tf_op jit(solution)/shard_map/reduce_scatter | solution.py:341
  652.9 331.6 %reduce-scatter.26.cloned.1.call-start = ((), (), s32[]{:S(2)}) async-start(), calls=%async_computation.29 | async-start | bytes 2228224 | tf_op jit(solution)/shard_map/reduce_scatter | solution.py:353
  662.7 386.4 %reduce-scatter.20.cloned.1.call-start = ((), (), s32[]{:S(2)}) async-start(), calls=%async_computation.26 | async-start | bytes 2228224 | tf_op jit(solution)/shard_map/reduce_scatter | solution.py:335
  678.2 404.6 %reduce-scatter.18.cloned.1.call-start = ((), (), s32[]{:S(2)}) async-start(), calls=%async_computation.25 | async-start | bytes 3145728 | tf_op jit(solution)/shard_map/reduce_scatter | solution.py:324
  686.4 438.4 %reduce-scatter.14.cloned.1.call-start = ((), (), s32[]{:S(2)}) async-start(), calls=%async_computation.21 | async-start | bytes 3145728 | tf_op jit(solution)/shard_map/reduce_scatter | solution.py:261
  693.1 389.7 %copy-start.19 = (bf16[512,1024]{1,0:T(8,128)(2,1)S(1)}, bf16[512,1024]{1,0:T(8,128)(2,1)}, u32[]{:S(2)}) copy-start(bf16[512,1024]{1,0:T(8,128)(2,1)} %param.15) | copy-start | bytes 3145732
  693.1 391.8 %copy-start.84 = (f32[1024]{0:T(1024)S(1)}, f32[1024]{0:T(1024)}, u32[]{:S(2)}) copy-start(f32[1024]{0:T(1024)} %get-tuple-element.13) | copy-start | bytes 12292
  693.1 431.7 %copy-start.3 = (f32[512,1024]{1,0:T(8,128)S(1)}, f32[512,1024]{1,0:T(8,128)}, u32[]{:S(2)}) copy-start(f32[512,1024]{1,0:T(8,128)} %copy-done.2) | copy-start | bytes 6291460
  693.1 431.7 %copy-start.74 = (f32[1024]{0:T(1024)S(1)}, f32[1024]{0:T(1024)}, u32[]{:S(2)}) copy-start(f32[1024]{0:T(1024)} %param.28) | copy-start | bytes 12292
  693.1 431.7 %copy-start.78 = (f32[512]{0:T(512)S(1)}, f32[512]{0:T(512)}, u32[]{:S(2)}) copy-start(f32[512]{0:T(512)} %copy-done.77) | copy-start | bytes 6148
  693.1 431.7 %copy-start.81 = (f32[512]{0:T(512)S(1)}, f32[512]{0:T(512)}, u32[]{:S(2)}) copy-start(f32[512]{0:T(512)} %copy-done.80) | copy-start | bytes 6148
  (100 other events, 996.8 us)
Sparse Core Ops, SparseCore 0:
  9.6 35.8 all-gather.13
  47.6 37.9 all-gather.17
  87.8 36.8 all-gather.15
  126.7 40.3 all-gather.19
  169.0 40.1 all-gather.21
  215.5 53.0 reduce-scatter.11
  271.1 45.3 all-gather.25
  318.7 31.9 all-gather.23
  353.2 45.1 all-gather.27
  399.9 31.9 all-gather.31
  434.4 45.1 all-gather.29
  500.7 53.0 reduce-scatter.15
  559.1 33.0 all-gather.33
  595.9 66.2 reduce-scatter.27
  665.8 65.2 reduce-scatter.29
  734.7 65.2 reduce-scatter.31
  803.4 56.2 reduce-scatter.23
  863.6 56.3 reduce-scatter.21
  923.8 60.5 reduce-scatter.25
  988.5 60.5 reduce-scatter.19
  1051.9 30.8 reduce-scatter.17
  1085.1 32.3 reduce-scatter.13
where the time goes:
time: 1140 us
  waiting for transfers between devices  810 us (71%)
  matrix products  176 us (15%)
  other arithmetic  61.5 us (5%)
  blocking collectives  49.6 us (4%)
  local copies, waits for them, and re-layouts  20.8 us (2%)
  between operations  16.4 us (1%)
    reduce_scatter x1, waiting for transfers between devices, per_device(): lax.psum_scatter(down_grad.astype(jnp.bfloat16), 'dp', scatter_dimension=...  67.2 us
    reduce_scatter x1, waiting for transfers between devices, per_device(): lax.psum_scatter(left_contract(first_rows, query_low).astype(jnp.bfloat16...  63 us
    reduce_scatter x1, waiting for transfers between devices, per_device(): lax.psum_scatter(out_weight_part.astype(jnp.bfloat16), 'dp', scatter_dime...  62.8 us
    reduce_scatter x1, waiting for transfers between devices, per_device(): lax.psum_scatter(left_contract(first_rows, key_low).astype(jnp.bfloat16),...  58.8 us
    reduce_scatter x1, waiting for transfers between devices, per_device(): lax.psum_scatter(left_contract(first_rows, value_low).astype(jnp.bfloat16...  58.1 us
    reduce_scatter x1, waiting for transfers between devices, per_device(): lax.psum_scatter(right_contract(gate_low, back_gate) + right_contract(up_...  53.2 us
    reduce_scatter x1, waiting for transfers between devices, per_device(): lax.psum_scatter(matmul(mixed_rows, full_out), 'tensor', scatter_dimensio...  52.4 us
    all_gather x1, waiting for transfers between devices, per_device(): lax.all_gather(down_weight, 'dp', axis=1, tiled=True)  47.8 us
  transfers between devices with their start and end apart: 22, of which 19 were waited for; matrix products, arithmetic and copies ran while one was open for 18% of the time, Pallas kernels for 0%

commit v1 on v0

--- a/solution.py
+++ b/solution.py
@@ -181,6 +181,69 @@
     )
 
 
+def swap_rows(values):
+    return lax.ppermute(values, "tensor", [(0, 1), (1, 0)])
+
+
+def row_blocks(own):
+    if lax.axis_size("tensor") == 2:
+        return [own, swap_rows(own)]
+    return [lax.all_gather(own, "tensor", axis=0, tiled=True)]
+
+
+def in_order(blocks):
+    if len(blocks) == 1:
+        return blocks[0]
+    own, other = blocks
+    first = lax.axis_index("tensor") == 0
+    return jnp.concatenate([jnp.where(first, own, other), jnp.where(first, other, own)], 0)
+
+
+def split_order(whole):
+    if lax.axis_size("tensor") != 2:
+        return [whole]
+    half = whole.shape[0] // 2
+    at = lax.axis_index("tensor") * half
+    return [
+        lax.dynamic_slice_in_dim(whole, at, half, 0),
+        lax.dynamic_slice_in_dim(whole, half - at, half, 0),
+    ]
+
+
+def sum_rows(blocks, product):
+    if len(blocks) == 1:
+        return lax.psum_scatter(
+            product(blocks[0]).astype(jnp.bfloat16), "tensor", scatter_dimension=0, tiled=True
+        ).astype(jnp.float32)
+    other = swap_rows(product(blocks[1]).astype(jnp.bfloat16))
+    return product(blocks[0]) + other.astype(jnp.float32)
+
+
+def gather_weights(parts):
+    return lax.all_gather(jnp.concatenate(parts, 1), "dp", axis=0, tiled=True)
+
+
+def side_by_side(parts):
+    return jnp.concatenate([part.astype(jnp.bfloat16) for part in parts], 1)
+
+
+def scatter_grads(whole):
+    summed = lax.psum_scatter(whole, "dp", scatter_dimension=0, tiled=True)
+    return summed.astype(jnp.float32)
+
+
+def sum_everywhere(values):
+    for axis in ("dp", "tensor"):
+        count = lax.axis_size(axis)
+        step = 1
+        while step < count:
+            values = values + lax.ppermute(
+                values, axis, [(index, index ^ step) for index in range(count)]
+            )
+            step *= 2
+    return values
+
+
 def per_device(
     tokens,
     segments,
@@ -198,33 +261,33 @@
     ffn_gain,
     out_grad,
 ):
-    tok_rows = tokens.shape[0]
+    tok_rows, width = tokens.shape
     head_dim = query_gain.shape[0]
     seq_rows = tok_rows * lax.axis_size("tensor")
-    q_heads = query_weight.shape[1] // head_dim
-    kv_heads = key_matrix.shape[1] // head_dim
+    q_cols, kv_cols = query_weight.shape[1], key_matrix.shape[1]
+    units = gate_weight.shape[1]
+    q_heads = q_cols // head_dim
+    kv_heads = kv_cols // head_dim
     heads_per_group = q_heads // kv_heads
     tile_rows = min(512, seq_rows)
     score_scale = head_dim ** (-0.5)
     inputs = tokens.astype(jnp.float32)
+    marks_places = jnp.stack([segments, positions], 1)
+    whole_marks = in_order(row_blocks(marks_places))
+    row_marks, row_places = whole_marks[:, 0], whole_marks[:, 1]
+    whole_tokens = in_order(row_blocks(tokens))
+    full_attn = gather_weights([query_weight, key_matrix, value_matrix, out_weight.T])
+    full_qkv = full_attn[:, : q_cols + 2 * kv_cols]
+    full_out = full_attn[:, q_cols + 2 * kv_cols :]
+    full_ffn = gather_weights([gate_weight, up_weight, down_weight.T])
+    full_query = full_qkv[:, :q_cols]
+    full_key = full_qkv[:, q_cols : q_cols + kv_cols]
+    full_value = full_qkv[:, q_cols + kv_cols :]
+    full_gate = full_ffn[:, :units]
+    full_up = full_ffn[:, units : 2 * units]
+    full_down = full_ffn[:, 2 * units :]
     unused_first, first_pull = jax.vjp(root_mean_norm, inputs, attn_gain)
-    whole_tokens = lax.all_gather(tokens, "tensor", axis=0, tiled=True)
-    inputs_whole = whole_tokens.astype(jnp.float32)
-    first_rows = root_mean_norm(inputs_whole, attn_gain).astype(jnp.bfloat16)
-    row_marks, row_places = (
-        lax.all_gather(segments, "tensor", axis=0, tiled=True),
-        lax.all_gather(positions, "tensor", axis=0, tiled=True),
-    )
-    weights = (
-        lax.all_gather(query_weight, "dp", axis=0, tiled=True),
-        lax.all_gather(key_matrix, "dp", axis=0, tiled=True),
-        lax.all_gather(value_matrix, "dp", axis=0, tiled=True),
-        lax.all_gather(out_weight, "dp", axis=1, tiled=True),
-        lax.all_gather(gate_weight, "dp", axis=0, tiled=True),
-        lax.all_gather(up_weight, "dp", axis=0, tiled=True),
-        lax.all_gather(down_weight, "dp", axis=1, tiled=True),
-    )
-    full_query, full_key, full_value, full_out, full_gate, full_up, full_down = weights
+    first_rows = root_mean_norm(whole_tokens.astype(jnp.float32), attn_gain).astype(jnp.bfloat16)
     cosine_table, sine_values = tables(row_places, head_dim)
 
     def head_prep(raw_cols, gain_row):
@@ -246,65 +309,44 @@
         query_rows, key_matrix_rows, value_matrix_rows, row_marks, tile_rows, score_scale
     )
     mixed_rows = mixed_heads.reshape(seq_rows, q_heads * head_dim)
-    hidden = inputs + lax.psum_scatter(
-        matmul(mixed_rows, full_out), "tensor", scatter_dimension=0, tiled=True
+    hidden = inputs + sum_rows(
+        split_order(mixed_rows), lambda rows: right_contract(rows, full_out)
     )
     second_own = root_mean_norm(hidden, ffn_gain)
-    second_rows = lax.all_gather(second_own.astype(jnp.bfloat16), "tensor", axis=0, tiled=True)
+    second_blocks = row_blocks(second_own.astype(jnp.bfloat16))
+    grad_blocks = row_blocks(out_grad)
     unused_second, second_pull = jax.vjp(root_mean_norm, hidden, ffn_gain)
-    gate_rows = matmul(second_rows, full_gate)
-    up_rows = matmul(second_rows, full_up)
-    activated, act_pull = jax.vjp(silu_product, gate_rows, up_rows)
-    act_low = activated.astype(jnp.bfloat16)
+    act_blocks, gate_lows, up_lows = [], [], []
+    for second_rows, grad_rows in zip(second_blocks, grad_blocks):
+        gate_rows = matmul(second_rows, full_gate)
+        up_rows = matmul(second_rows, full_up)
+        activated, act_pull = jax.vjp(silu_product, gate_rows, up_rows)
+        act_blocks.append(activated.astype(jnp.bfloat16))
+        grad_gate, grad_up = act_pull(matmul(grad_rows, full_down))
+        gate_lows.append(grad_gate.astype(jnp.bfloat16))
+        up_lows.append(grad_up.astype(jnp.bfloat16))
+    grad_second = sum_rows(
+        list(zip(gate_lows, up_lows)),
+        lambda lows: right_contract(lows[0], full_gate) + right_contract(lows[1], full_up),
+    )
     layer_out = (
-        hidden
-        + lax.psum_scatter(
-            matmul(act_low, full_down).astype(jnp.bfloat16),
-            "tensor",
-            scatter_dimension=0,
-            tiled=True,
-        ).astype(jnp.float32)
+        hidden + sum_rows(act_blocks, lambda rows: right_contract(rows, full_down))
     ).astype(jnp.bfloat16)
-    grad_rows = lax.all_gather(out_grad, "tensor", axis=0, tiled=True)
-    back_weights = (
-        lax.all_gather(query_weight, "dp", axis=0, tiled=True),
-        lax.all_gather(key_matrix, "dp", axis=0, tiled=True),
-        lax.all_gather(value_matrix, "dp", axis=0, tiled=True),
-        lax.all_gather(out_weight, "dp", axis=1, tiled=True),
-        lax.all_gather(gate_weight, "dp", axis=0, tiled=True),
-        lax.all_gather(up_weight, "dp", axis=0, tiled=True),
-        lax.all_gather(down_weight, "dp", axis=1, tiled=True),
-    )
-    back_query, back_key, back_value, back_out, back_gate, back_up, back_down = back_weights
-    grad_act = right_contract(grad_rows, back_down)
-    down_grad = left_contract(act_low, grad_rows)
-    grad_gate, grad_up = act_pull(grad_act)
-    gate_low = grad_gate.astype(jnp.bfloat16)
-    up_low = grad_up.astype(jnp.bfloat16)
-    gate_grad = left_contract(second_rows, gate_low)
-    up_grad = left_contract(second_rows, up_low)
-    grad_second = lax.psum_scatter(
-        right_contract(gate_low, back_gate) + right_contract(up_low, back_up),
-        "tensor",
-        scatter_dimension=0,
-        tiled=True,
-    )
-    ffn_grads = (
-        lax.psum_scatter(
-            gate_grad.astype(jnp.bfloat16), "dp", scatter_dimension=0, tiled=True
-        ).astype(jnp.float32),
-        lax.psum_scatter(
-            up_grad.astype(jnp.bfloat16), "dp", scatter_dimension=0, tiled=True
-        ).astype(jnp.float32),
-        lax.psum_scatter(
-            down_grad.astype(jnp.bfloat16), "dp", scatter_dimension=1, tiled=True
-        ).astype(jnp.float32),
-    )
+    second_rows = jnp.concatenate(second_blocks, 0)
+    ffn_parts = side_by_side(
+        [
+            left_contract(second_rows, jnp.concatenate(gate_lows, 0)),
+            left_contract(second_rows, jnp.concatenate(up_lows, 0)),
+            left_contract(jnp.concatenate(grad_blocks, 0), jnp.concatenate(act_blocks, 0)),
+        ]
+    )
+    ffn_grads = scatter_grads(ffn_parts)
+    grad_second = lax.optimization_barrier((grad_second, ffn_parts))[0]
     grad_norm, ffn_gain_part = second_pull(grad_second)
     grad_hidden = out_grad.astype(jnp.float32) + grad_norm
-    attn_rows = lax.all_gather(grad_hidden.astype(jnp.bfloat16), "tensor", axis=0, tiled=True)
-    grad_mixed = right_contract(attn_rows, back_out).astype(jnp.bfloat16)
-    out_weight_part = left_contract(mixed_rows, attn_rows)
+    attn_rows = in_order(row_blocks(grad_hidden.astype(jnp.bfloat16)))
+    grad_mixed = matmul(attn_rows, full_out).astype(jnp.bfloat16)
+    out_weight_part = left_contract(attn_rows, mixed_rows)
     grad_query, grad_key, grad_value = attend_backward(
         query_rows,
         key_matrix_rows,
@@ -318,61 +360,39 @@
     )
     query_back, query_gain_part = query_pull(grad_query.reshape(seq_rows, q_heads, head_dim))
     key_back, key_gain_part = key_pull(grad_key)
-    query_low = query_back.astype(jnp.bfloat16)
-    key_low = key_back.astype(jnp.bfloat16)
-    value_low = grad_value.reshape(seq_rows, kv_heads * head_dim).astype(jnp.bfloat16)
-    grad_first = lax.psum_scatter(
-        (
-            right_contract(query_low, back_query)
-            + right_contract(key_low, back_key)
-            + right_contract(value_low, back_value)
-        ).astype(jnp.bfloat16),
-        "tensor",
-        scatter_dimension=0,
-        tiled=True,
-    ).astype(jnp.float32)
-    attn_grads = (
-        lax.psum_scatter(
-            left_contract(first_rows, query_low).astype(jnp.bfloat16),
-            "dp",
-            scatter_dimension=0,
-            tiled=True,
-        ).astype(jnp.float32),
-        lax.psum_scatter(
-            left_contract(first_rows, key_low).astype(jnp.bfloat16),
-            "dp",
-            scatter_dimension=0,
-            tiled=True,
-        ).astype(jnp.float32),
-        lax.psum_scatter(
-            left_contract(first_rows, value_low).astype(jnp.bfloat16),
-            "dp",
-            scatter_dimension=0,
-            tiled=True,
-        ).astype(jnp.float32),
-        lax.psum_scatter(
-            out_weight_part.astype(jnp.bfloat16), "dp", scatter_dimension=1, tiled=True
-        ).astype(jnp.float32),
+    qkv_low = jnp.concatenate(
+        [
+            query_back.astype(jnp.bfloat16),
+            key_back.astype(jnp.bfloat16),
+            grad_value.reshape(seq_rows, kv_cols).astype(jnp.bfloat16),
+        ],
+        1,
+    )
+    grad_first = sum_rows(
+        split_order(qkv_low), lambda rows: right_contract(rows, full_qkv)
+    )
+    attn_grads = scatter_grads(
+        side_by_side([left_contract(first_rows, qkv_low), out_weight_part])
     )
     grad_inputs, attn_gain_part = first_pull(grad_first)
     tokens_grad = grad_hidden + grad_inputs
-    gain_grads = lax.psum(
-        (attn_gain_part, query_gain_part, key_gain_part, ffn_gain_part), ("dp", "tensor")
+    gain_grads = sum_everywhere(
+        jnp.concatenate([attn_gain_part, ffn_gain_part, query_gain_part, key_gain_part])
     )
     return (
         layer_out,
         tokens_grad,
-        attn_grads[0],
-        attn_grads[1],
-        attn_grads[2],
-        attn_grads[3],
-        ffn_grads[0],
-        ffn_grads[1],
-        ffn_grads[2],
-        gain_grads[0],
-        gain_grads[1],
-        gain_grads[2],
-        gain_grads[3],
+        attn_grads[:, :q_cols],
+        attn_grads[:, q_cols : q_cols + kv_cols],
+        attn_grads[:, q_cols + kv_cols : q_cols + 2 * kv_cols],
+        attn_grads[:, q_cols + 2 * kv_cols :].T,
+        ffn_grads[:, :units],
+        ffn_grads[:, units : 2 * units],
+        ffn_grads[:, 2 * units :].T,
+        gain_grads[:width],
+        gain_grads[2 * width : 2 * width + head_dim],
+        gain_grads[2 * width + head_dim :],
+        gain_grads[width : 2 * width],
     )
 
 

time: 1140 us -> 566 us (0.50)
  waiting for transfers between devices: 810 us -> 283 us
  blocking collectives: 49.6 us -> 0 us
  matrix products: 176 us -> 163 us
  starting transfers between devices: 2.14 us -> 14.8 us
    reduce_scatter x11 -> x2, waiting for transfers between devices: 484 us -> 126 us  [scatter_grads(): summed = lax.psum_scatter(whole, 'dp', scatter_dimension=0, tiled=True)]
    all_gather x11 -> x2, waiting for transfers between devices: 321 us -> 28 us  [gather_weights(): return lax.all_gather(jnp.concatenate(parts, 1), 'dp', axis=0, tiled=True)]
    ppermute x0 -> x14, waiting for transfers between devices: none -> 128 us  [the longest x9 120 us: swap_rows(): return lax.ppermute(values, 'tensor', [(0, 1), (1, 0)])]
    psum x1 -> x0, blocking collectives: 39.8 us -> none  [per_device(): lax.psum((attn_gain_part, query_gain_part, key_gain_part, ffn_gain_part),...]
    concatenate x0 -> x6, other arithmetic: none -> 16.3 us  [the longest x2 9.83 us: side_by_side(): return jnp.concatenate([part.astype(jnp.bfloat16) for part in parts], 1)]
    ppermute x0 -> x14, starting transfers between devices: none -> 14.7 us  [the longest x9 10.8 us: swap_rows(): return lax.ppermute(values, 'tensor', [(0, 1), (1, 0)])]
    dot_general x7 -> x5, matrix products: 34.8 us -> 25.3 us  [left_contract(): lax.dot_general(left_side, right_side, (((0,), (0,)), ((), ())), preferre...]
    dot_general x7 -> x10, matrix products: 42.6 us -> 39.3 us  [matmul(): return jnp.dot(left_side, right_side, preferred_element_type=jnp.float32)]
  transfers between devices with their start and end apart: 22 -> 18, of which waited for: 19 -> 13; matrix products, arithmetic and copies ran while one was open for 18% -> 25% of each run, Pallas kernels for 0% -> 0%
where the time goes in v1:
time: 566 us; the launch traced here: 557 us
  waiting for transfers between devices  283 us (50%)
  matrix products  163 us (29%)
  other arithmetic  55.6 us (10%)
  local copies, waits for them, and re-layouts  24.3 us (4%)
  between operations  15.9 us (3%)
  starting transfers between devices  14.8 us (3%)
    reduce_scatter x2, waiting for transfers between devices, scatter_grads(): summed = lax.psum_scatter(whole, 'dp', scatter_dimension=0, tiled=True)  126 us
    ppermute x9, waiting for transfers between devices, swap_rows(): return lax.ppermute(values, 'tensor', [(0, 1), (1, 0)])  120 us
    dot_general x10, matrix products, matmul(): return jnp.dot(left_side, right_side, preferred_element_type=jnp.float32)  39.3 us
    dot_general x10, matrix products, right_contract(): lax.dot_general(left_side, right_side, (((1,), (1,)), ((), ())), preferre...  34.1 us
    all_gather x2, waiting for transfers between devices, gather_weights(): return lax.all_gather(jnp.concatenate(parts, 1), 'dp', axis=0, tiled=True)  28 us
    dot_general x5, matrix products, left_contract(): lax.dot_general(left_side, right_side, (((0,), (0,)), ((), ())), preferre...  25.3 us
    dot_general x3, matrix products, attend_forward(): jnp.einsum('gsqk,kgd->qgsd', low_part, v_block, preferred_element_type=jn...  16.5 us
    dot_general x3, matrix products, attend_backward(): jnp.einsum('qgsd,kgd->gsqk', grad_block, v_block, preferred_element_type=...  12.5 us
  transfers between devices with their start and end apart: 18, of which 13 were waited for; matrix products, arithmetic and copies ran while one was open for 25% of the time, Pallas kernels for 0%

profile of v1, /device:TPU:0, one launch (start us, length us, event | category | flops | bytes accessed | tf_op | source)
XLA Modules:
  0.0 556.7 jit_solution(7334820916938263339)
XLA Ops:
  15.0 22.8 %collective-permute-done.1 = s32[512,2]{0,1:T(2,128)S(1)} collective-permute-done((s32[512,2]{0,1:T(2,128)S(1)}, s32[512,2]{0,1:T(2,128)S(1)}, u32[]{:S(2)}, u32[]{:S(2)}) %collective-permute-start.1) | collective-permute-done | bytes 4128 | tf_op jit(solution)/shard_map/ppermute | solution.py:185
  47.4 28.0 %all-gather.3.cloned.1.call-done = bf16[1024,3072]{1,0:T(8,128)(2,1)} async-done(((bf16[64,3072]{1,0:T(8,128)(2,1)}), bf16[1024,3072]{1,0:T(8,128)(2,1)}) %all-gather.3.cloned.1.call-update) | async-done | bytes 6291472 | tf_op jit(solution)/shard_map/all_gather | solution.py:223
  75.5 4.3 multiply_reduce_fusion.8
  81.7 5.9 %multiply_reduce_fusion.2 = (f32[1024,8]{0,1:T(8,128)S(1)}, f32[1024,1024]{0,1:T(8,128)S(1)}) fusion(bf16[1024,3072]{1,0:T(8,128)(2,1)} %all-gather.3.cloned.1.call-done, f32[1024]{0:T(1024)S(1)} %copy-done.75, f32[1024]{0:T(1024)S(1)} %add_rsqrt_fusion, bf16[512,1024]{1,0:T(8,128)(2,1)} %copy-done.38, bf16[512,1024]{1,0:T(8,128)(2,1)} %copy-done.35), kind=kOutput, calls=%fused_computation.52 | convolution fusion | flops 2156912640 | bytes 8429568 | tf_op jit(solution)/shard_map/dot_general | solution.py:36
  102.8 4.1 select_reduce_fusion
  118.7 4.0 fusion.99
  124.8 24.1 %collective-permute-done.2 = bf16[512,1024]{1,0:T(8,128)(2,1)} collective-permute-done((bf16[512,1024]{1,0:T(8,128)(2,1)S(1)}, bf16[512,1024]{1,0:T(8,128)(2,1)}, u32[]{:S(2)}, u32[]{:S(2)}) %collective-permute-start.2) | collective-permute-done | bytes 1048608 | tf_op jit(solution)/shard_map/ppermute | solution.py:185
  148.9 3.8 multiply_reduce_fusion.7
  154.4 7.8 %add_bitcast_fusion.1 = f32[512,4,2,128]{0,3,2,1:T(8,128)} fusion(f32[4,128,2,512]{3,1,2,0:T(8,128)S(1)} %copy-done.46, bf16[512,4,128,1]{0,2,3,1:T(8,128)(2,1)S(1)} %bitcast.310, f32[4,2,512]{2,1,0:T(2,128)S(1)} %log_add_fusion.1, f32[4,512,512,2]{2,1,3,0:T(8,128)} %copy-done.4, pred[512,512]{0,1:T(8,128)(4,1)S(1)} %copy-done.33), kind=kOutput, calls=%fused_computation.132 | convolution fusion | flops 554172416 | bytes 13385728 | tf_op jit(solution)/shard_map/gsqk,kgd->qgsd/dot_general | solution.py:103
  162.2 9.1 %collective-permute-done.5 = bf16[512,1024]{1,0:T(8,128)(2,1)} collective-permute-done((bf16[512,1024]{1,0:T(8,128)(2,1)}, bf16[512,1024]{1,0:T(8,128)(2,1)}, u32[]{:S(2)}, u32[]{:S(2)}) %collective-permute-start.5) | collective-permute-done | bytes 1048608 | tf_op jit(solution)/shard_map/ppermute | solution.py:185
  171.3 4.1 convolution_bitcast_fusion
  175.5 17.7 %collective-permute-done.3 = bf16[512,1024]{1,0:T(8,128)(2,1)} collective-permute-done((bf16[512,1024]{1,0:T(8,128)(2,1)S(1)}, bf16[512,1024]{1,0:T(8,128)(2,1)}, u32[]{:S(2)}, u32[]{:S(2)}) %collective-permute-start.3) | collective-permute-done | bytes 1048608 | tf_op jit(solution)/shard_map/ppermute | solution.py:185
  196.2 4.7 fusion.31
  215.0 5.8 %convolution_convert_fusion.1 = bf16[1024,1536]{1,0:T(8,128)(2,1)S(1)} fusion(bf16[512,1536]{1,0:T(8,128)(2,1)S(1)} %get-tuple-element.29, bf16[512,1536]{1,0:T(8,128)(2,1)S(1)} %get-tuple-element.26, bf16[512,1024]{1,0:T(8,128)(2,1)} %collective-permute-done.3, bf16[512,1024]{1,0:T(8,128)(2,1)S(1)} %multiply_convert_fusion.4), kind=kOutput, calls=%fused_computation.60 | convolution fusion | flops 3233284096 | bytes 8388608 | tf_op jit(solution)/shard_map/dot_general | solution.py:40
  220.9 5.0 convolution_convert_fusion.2
  225.9 5.8 %convolution_convert_fusion = bf16[1024,1536]{1,0:T(8,128)(2,1)S(1)} fusion(bf16[512,1536]{1,0:T(8,128)(2,1)S(1)} %get-tuple-element.30, bf16[512,1536]{1,0:T(8,128)(2,1)S(1)} %get-tuple-element.27, bf16[512,1024]{1,0:T(8,128)(2,1)} %collective-permute-done.5, bf16[512,1024]{1,0:T(8,128)(2,1)} %param.29), kind=kOutput, calls=%fused_computation.59 | convolution fusion | flops 3233284096 | bytes 8388608 | tf_op jit(solution)/shard_map/dot_general | solution.py:40
  234.8 5.0 pad_maximum_fusion
  239.9 5.2 convert_add_fusion.2
  248.3 5.3 fusion.14
  257.1 14.9 %collective-permute-done.7 = bf16[512,1024]{1,0:T(8,128)(2,1)S(1)} collective-permute-done((bf16[512,1024]{1,0:T(8,128)(2,1)S(1)}, bf16[512,1024]{1,0:T(8,128)(2,1)S(1)}, u32[]{:S(2)}, u32[]{:S(2)}) %collective-permute-start.7) | collective-permute-done | bytes 1048608 | tf_op jit(solution)/shard_map/ppermute | solution.py:185
  272.1 6.3 %fusion.19 = (f32[4,2,1024]{2,1,0:T(2,128)S(1)}, bf16[1024,1024]{0,1:T(8,128)(2,1)S(1)}) fusion(f32[512,4,2,128]{0,3,2,1:T(8,128)S(1)} %add_bitcast_fusion, f32[512,4,2,128]{0,3,2,1:T(8,128)S(1)} %copy-done.85, bf16[1024,3072]{1,0:T(8,128)(2,1)} %all-gather.3.cloned.1.call-done, bf16[512,1024]{1,0:T(8,128)(2,1)S(1)} %get-tuple-element.40, ...), kind=kOutput, calls=%fused_computation.43 | convolution fusion | flops 2156912640 | bytes 10518528 | tf_op jit(solution)/shard_map/dot_general | solution.py:36
  290.2 5.7 %fusion.3 = bf16[4,2,512,512]{2,3,1,0:T(8,128)(2,1)S(1)} fusion(f32[4,2,512]{2,1,0:T(2,128)S(1)} %get-tuple-element.56, bf16[512,4,128,1]{0,2,3,1:T(8,128)(2,1)S(1)} %bitcast.312, bf16[512,4,2,128]{0,3,2,1:T(8,128)(2,1)} %bitcast.307, f32[4,2,512]{2,1,0:T(2,128)S(1)} %log_add_fusion, f32[4,512,512,2]{2,1,3,0:T(8,128)S(1)} %bitcast.285, ...), kind=kOutput, calls=%fused_computation.6 | convolution fusion | flops 551550976 | bytes 14450688 | tf_op jit(solution)/shard_map/qgsd,kgd->gsqk/dot_general | solution.py:152
  299.4 3.7 convolution_convert_fusion.4
  323.7 3.8 multiply_bitcast_fusion
  337.2 5.0 convolution_convert_fusion.3
  342.2 4.8 pad_maximum_fusion.1
  350.2 5.8 %fusion.94 = bf16[512,1024]{1,0:T(8,128)(2,1)S(1)} fusion(bf16[1024,3072]{1,0:T(8,128)(2,1)} %all-gather.3.cloned.1.call-done, bf16[1024,2048]{0,1:T(8,128)(2,1)S(1)} %pad_maximum_fusion.3, s32[]{:T(128)S(6)} %select_n.93), kind=kOutput, calls=%fused_computation.172 | convolution fusion | flops 2148007936 | bytes 7340036 | tf_op jit(solution)/shard_map/dot_general | solution.py:46
  360.4 21.8 %collective-permute-done.8 = bf16[512,1024]{1,0:T(8,128)(2,1)S(1)} collective-permute-done((bf16[512,1024]{1,0:T(8,128)(2,1)S(1)}, bf16[512,1024]{1,0:T(8,128)(2,1)S(1)}, u32[]{:S(2)}, u32[]{:S(2)}) %collective-permute-start.8) | collective-permute-done | bytes 1048608 | tf_op jit(solution)/shard_map/ppermute | solution.py:185
  386.7 3.7 collective-permute-done.10
  391.7 10.0 %collective-permute-done.4 = bf16[512,1024]{1,0:T(8,128)(2,1)S(1)} collective-permute-done((bf16[512,1024]{1,0:T(8,128)(2,1)S(1)}, bf16[512,1024]{1,0:T(8,128)(2,1)S(1)}, u32[]{:S(2)}, u32[]{:S(2)}) %collective-permute-start.4) | collective-permute-done | bytes 1048608 | tf_op jit(solution)/shard_map/ppermute | solution.py:185
  414.5 16.3 %reduce-scatter.3.cloned.1.call-done = bf16[64,3072]{1,0:T(8,128)(2,1)} async-done(((bf16[1024,3072]{1,0:T(8,128)(2,1)}), bf16[64,3072]{1,0:T(8,128)(2,1)}) %reduce-scatter.3.cloned.1.call-update) | async-done | bytes 393232 | tf_op jit(solution)/shard_map/reduce_scatter | solution.py:231
  435.8 110.0 %reduce-scatter.5.cloned.1.call-done = bf16[64,4608]{1,0:T(8,128)(2,1)} async-done(((bf16[1024,4608]{1,0:T(8,128)(2,1)}), bf16[64,4608]{1,0:T(8,128)(2,1)}) %reduce-scatter.5.cloned.1.call-update) | async-done | bytes 589840 | tf_op jit(solution)/shard_map/reduce_scatter | solution.py:231
  (335 shorter events, 156.4 us)
Async XLA Ops:
  7.2 37.4 %copy-start.14 = (bf16[512,1024]{1,0:T(8,128)(2,1)S(1)}, bf16[512,1024]{1,0:T(8,128)(2,1)}, u32[]{:S(2)}) copy-start(bf16[512,1024]{1,0:T(8,128)(2,1)} %param.15) | copy-start | bytes 3145732
  7.2 68.3 %all-gather.3.cloned.1.call-start = ((), (), s32[]{:S(2)}) async-start(), calls=%async_computation.2 | async-start | bytes 6684672 | tf_op jit(solution)/shard_map/all_gather | solution.py:223
  9.1 162.2 %all-gather.5.cloned.1.call-start = ((), (), s32[]{:S(2)}) async-start(), calls=%async_computation.3 | async-start | bytes 10027008 | tf_op jit(solution)/shard_map/all_gather | solution.py:223
  11.2 419.6 %reduce-scatter.3.cloned.1.call-start = ((), (), s32[]{:S(2)}) async-start(), calls=%async_computation.4 | async-start | bytes 6684672 | tf_op jit(solution)/shard_map/reduce_scatter | solution.py:231
  11.3 33.3 %collective-permute-start = (bf16[512,1024]{1,0:T(8,128)(2,1)}, bf16[512,1024]{1,0:T(8,128)(2,1)}, u32[]{:S(2)}, u32[]{:S(2)}) collective-permute-start(bf16[512,1024]{1,0:T(8,128)(2,1)} %param.15), channel_id=1, source_target_pairs={{0,1},{1,0},{2,3},{3,2},{4,5},{5,4},{6,7},{7,6},{8,9},{9,8},{10,11... | collective-permute-start | bytes 3145736 | tf_op jit(solution)/shard_map/ppermute | solution.py:185
  15.0 22.8 %collective-permute-start.1 = (s32[512,2]{0,1:T(2,128)S(1)}, s32[512,2]{0,1:T(2,128)S(1)}, u32[]{:S(2)}, u32[]{:S(2)}) collective-permute-start(s32[512,2]{0,1:T(2,128)S(1)} %pad_add_fusion.2), channel_id=1, source_target_pairs={{0,1},{1,0},{2,3},{3,2},{4,5},{5,4},{6,7},{7,6},{8,9},{9,8},{10,11... | collective-permute-start | bytes 12296 | tf_op jit(solution)/shard_map/ppermute | solution.py:185
  42.1 33.3 %copy-start.75 = (f32[1024]{0:T(1024)S(1)}, f32[1024]{0:T(1024)}, u32[]{:S(2)}) copy-start(f32[1024]{0:T(1024)} %param.25) | copy-start | bytes 12292
  45.9 33.8 %copy-start.35 = (bf16[512,1024]{1,0:T(8,128)(2,1)}, bf16[512,1024]{1,0:T(8,128)(2,1)S(1)}, u32[]{:S(2)}) copy-start(bf16[512,1024]{1,0:T(8,128)(2,1)S(1)} %get-tuple-element.45) | copy-start | bytes 3145732
  47.4 59.5 %copy-start.77 = (f32[1024]{0:T(1024)}, f32[1024]{0:T(1024)S(1)}, u32[]{:S(2)}) copy-start(f32[1024]{0:T(1024)S(1)} %add_rsqrt_fusion) | copy-start | bytes 12292
  122.7 26.2 %collective-permute-start.2 = (bf16[512,1024]{1,0:T(8,128)(2,1)S(1)}, bf16[512,1024]{1,0:T(8,128)(2,1)}, u32[]{:S(2)}, u32[]{:S(2)}) collective-permute-start(bf16[512,1024]{1,0:T(8,128)(2,1)S(1)} %fusion.99), channel_id=1, source_target_pairs={{0,1},{1,0},{2,3},{3,2},{4,5},{5,4},{6,7},{7,6},{8,9},{9,8},{10,11... | collective-permute-start | bytes 3145736 | tf_op jit(solution)/shard_map/ppermute | solution.py:185
  124.2 47.1 %collective-permute-start.5 = (bf16[512,1024]{1,0:T(8,128)(2,1)}, bf16[512,1024]{1,0:T(8,128)(2,1)}, u32[]{:S(2)}, u32[]{:S(2)}) collective-permute-start(bf16[512,1024]{1,0:T(8,128)(2,1)} %param.29), channel_id=1, source_target_pairs={{0,1},{1,0},{2,3},{3,2},{4,5},{5,4},{6,7},{7,6},{8,9},{9,8},{10,11... | collective-permute-start | bytes 3145736 | tf_op jit(solution)/shard_map/ppermute | solution.py:185
  124.8 27.9 %copy-start.68 = (f32[1024]{0:T(1024)S(1)}, f32[1024]{0:T(1024)}, u32[]{:S(2)}) copy-start(f32[1024]{0:T(1024)} %param.28) | copy-start | bytes 12292
  124.8 29.6 %copy-start.33 = (pred[512,512]{0,1:T(8,128)(4,1)S(1)}, pred[512,512]{0,1:T(8,128)(4,1)}, u32[]{:S(2)}) copy-start(pred[512,512]{0,1:T(8,128)(4,1)} %get-tuple-element.67) | copy-start | bytes 786436
  124.8 29.6 %copy-start.46 = (f32[4,128,2,512]{3,1,2,0:T(8,128)S(1)}, f32[4,128,2,512]{3,1,2,0:T(8,128)}, u32[]{:S(2)}) copy-start(f32[4,128,2,512]{3,1,2,0:T(8,128)} %copy-done.45) | copy-start | bytes 6291460
  124.8 29.6 %copy-start.58 = (bf16[512,512]{0,1:T(8,128)(2,1)S(1)}, bf16[512,512]{0,1:T(8,128)(2,1)}, u32[]{:S(2)}) copy-start(bf16[512,512]{0,1:T(8,128)(2,1)} %copy-done.57) | copy-start | bytes 1572868
  153.0 40.2 %collective-permute-start.3 = (bf16[512,1024]{1,0:T(8,128)(2,1)S(1)}, bf16[512,1024]{1,0:T(8,128)(2,1)}, u32[]{:S(2)}, u32[]{:S(2)}) collective-permute-start(bf16[512,1024]{1,0:T(8,128)(2,1)S(1)} %multiply_convert_fusion.4), channel_id=1, source_target_pairs={{0,1},{1,0},{2,3},{3,2},{4,5},{5,4},{6,7},{7,6},{8,9},{9,8},{10,11... | collective-permute-start | bytes 3145736 | tf_op jit(solution)/shard_map/ppermute | solution.py:185
  171.3 21.8 %copy-start.79 = (bf16[1024,4608]{1,0:T(8,128)(2,1)S(1)}, bf16[1024,4608]{1,0:T(8,128)(2,1)}, u32[]{:S(2)}) copy-start(bf16[1024,4608]{1,0:T(8,128)(2,1)} %all-gather.5.cloned.1.call-done) | copy-start | bytes 28311556
  200.8 25.1 %copy-start.82 = (bf16[512,1536]{1,0:T(8,128)(2,1)}, bf16[512,1536]{1,0:T(8,128)(2,1)S(1)}, u32[]{:S(2)}) copy-start(bf16[512,1536]{1,0:T(8,128)(2,1)S(1)} %get-tuple-element.30) | copy-start | bytes 4718596
  205.5 34.4 %collective-permute-start.6 = (bf16[512,1024]{1,0:T(8,128)(2,1)}, bf16[512,1024]{1,0:T(8,128)(2,1)}, u32[]{:S(2)}, u32[]{:S(2)}) collective-permute-start(bf16[512,1024]{1,0:T(8,128)(2,1)} %add_convert_fusion), channel_id=1, source_target_pairs={{0,1},{1,0},{2,3},{3,2},{4,5},{5,4},{6,7},{7,6},{8,9},{9,8},{10,11... | collective-permute-start | bytes 3145736 | tf_op jit(solution)/shard_map/ppermute | solution.py:185
  247.7 24.3 %collective-permute-start.7 = (bf16[512,1024]{1,0:T(8,128)(2,1)S(1)}, bf16[512,1024]{1,0:T(8,128)(2,1)S(1)}, u32[]{:S(2)}, u32[]{:S(2)}) collective-permute-start(bf16[512,1024]{1,0:T(8,128)(2,1)S(1)} %fusion.172), channel_id=1, source_target_pairs={{0,1},{1,0},{2,3},{3,2},{4,5},{5,4},{6,7},{7,6},{8,9},{9,8},{10,11... | collective-permute-start | bytes 3145736 | tf_op jit(solution)/shard_map/ppermute | solution.py:185
  347.0 198.8 %reduce-scatter.5.cloned.1.call-start = ((), (), s32[]{:S(2)}) async-start(), calls=%async_computation.5 | async-start | bytes 10027008 | tf_op jit(solution)/shard_map/reduce_scatter | solution.py:231
  347.6 34.6 %slice-start.9 = ((s8[6291456]{0:T(1024)(128)(4,1)}), s8[4194304]{0:T(1024)(128)(4,1)S(1)}, s32[]{:S(2)}) async-start(s8[6291456]{0:T(1024)(128)(4,1)} %bitcast.328), calls=%async_computation.15 | async-start | bytes 8388608
  350.2 32.0 %slice-start.10 = ((s8[6291456]{0:T(1024)(128)(4,1)}), s8[2097152]{0:T(1024)(128)(4,1)S(1)}, s32[]{:S(2)}) async-start(s8[6291456]{0:T(1024)(128)(4,1)} %bitcast.328), calls=%async_computation.16 | async-start | bytes 4194304
  356.0 26.2 %collective-permute-start.8 = (bf16[512,1024]{1,0:T(8,128)(2,1)S(1)}, bf16[512,1024]{1,0:T(8,128)(2,1)S(1)}, u32[]{:S(2)}, u32[]{:S(2)}) collective-permute-start(bf16[512,1024]{1,0:T(8,128)(2,1)S(1)} %fusion.94), channel_id=1, source_target_pairs={{0,1},{1,0},{2,3},{3,2},{4,5},{5,4},{6,7},{7,6},{8,9},{9,8},{10,11... | collective-permute-start | bytes 3145736 | tf_op jit(solution)/shard_map/ppermute | solution.py:185
  358.9 42.9 %copy-start.81 = (bf16[512,1536]{1,0:T(8,128)(2,1)S(1)}, bf16[512,1536]{1,0:T(8,128)(2,1)}, u32[]{:S(2)}) copy-start(bf16[512,1536]{1,0:T(8,128)(2,1)} %copy-done.80) | copy-start | bytes 4718596
  358.9 42.9 %collective-permute-start.4 = (bf16[512,1024]{1,0:T(8,128)(2,1)S(1)}, bf16[512,1024]{1,0:T(8,128)(2,1)S(1)}, u32[]{:S(2)}, u32[]{:S(2)}) collective-permute-start(bf16[512,1024]{1,0:T(8,128)(2,1)S(1)} %fusion.102), channel_id=1, source_target_pairs={{0,1},{1,0},{2,3},{3,2},{4,5},{5,4},{6,7},{7,6},{8,9},{9,8},{10,11... | collective-permute-start | bytes 3145736 | tf_op jit(solution)/shard_map/ppermute | solution.py:185
  385.2 1.2 collective-permute-start.9
  386.4 3.9 collective-permute-start.10
  390.3 19.4 %copy-start.10 = (f32[512,1024]{1,0:T(8,128)S(1)}, f32[512,1024]{1,0:T(8,128)}, u32[]{:S(2)}) copy-start(f32[512,1024]{1,0:T(8,128)} %copy-done.9) | copy-start | bytes 6291460
  390.3 14.2 %collective-permute-start.11 = (f32[2304]{0:T(1024)S(1)}, f32[2304]{0:T(1024)S(1)}, u32[]{:S(2)}, u32[]{:S(2)}) collective-permute-start(f32[2304]{0:T(1024)S(1)} %add.274), channel_id=1, source_target_pairs={{0,8},{2,10},{4,12},{6,14},{8,0},{10,2},{12,4},{14,6},{16,24},{18,... | collective-permute-start | bytes 27656 | tf_op jit(solution)/shard_map/ppermute | solution.py:240
  404.6 4.8 collective-permute-start.12
  409.3 4.0 collective-permute-start.13
  (84 other events, 386.4 us)
Sparse Core Ops, SparseCore 0:
  10.9 64.5 all-gather.2
  77.7 80.0 all-gather.4
  347.1 83.6 reduce-scatter.2
  435.3 110.4 reduce-scatter.4
